TPU v7x, 32 devices: a whole 2x2x4 slice. The times are simulated.
32 devices in a mesh: grp: 2 (over x), head: 8 (over z, y), item: 2 (over core).
Axes of the slice: x: 2, y: 2, z: 4, core: 2. Of those that a mesh axis runs over, the one named last changes fastest.
Arguments:
- passage_states: bfloat16 [4096, 8192], P(('grp', 'item'), 'head'), parts along dimension 0
- question_states: bfloat16 [2048, 8192], P(('grp', 'item'), 'head'), parts along dimension 0
- norm_gain: float32 [8192], P('head'), may hold values from 0.1 to 1.9
- query_weight: bfloat16 [8192, 8192], P(None, 'head')
- kv_weight: bfloat16 [8192, 2048], P('head')
- out_weight: bfloat16 [8192, 8192], P('head'), may hold values from -0.09375 to 0.09375
- passage_ids: int32 [16, 4], P(('grp', 'item')), parts along dimension 0, may hold values from 0 to 7, all different within a row
- slot_offsets: int32 [16, 4], P(('grp', 'item')), parts along dimension 0, may hold values from 0 to 768
Outputs:
- passage_kv: bfloat16 [4096, 2048], P(('grp', 'item'), 'head'), parts along dimension 0
- question_out: bfloat16 [2048, 8192], P(('grp', 'item'), 'head'), parts along dimension 0
There are 2 independent parts, one for each index of `grp`. A program takes and returns all parts, laid end to end along the dimension named above; an argument that names none is the same for every part. Nothing has to cross between parts.
Inputs may be any that keep to these rules, and one draw needn't show every extreme that they name: `passage_ids`: each request names 4 different passages and every passage is named by some request.
All inputs are finite; a program needn't handle non-finite values.
Results may differ from a plain program's by a relative error of at most 0.0055.
Values may be sent and summed in bfloat16 or wider, within the bound.
No kernel may reach another device: no remote copies, remote signals or barrier semaphores. Data moves between devices by JAX's collectives and lax.ppermute only.
A program may use at most 192 MiB of HBM per device.

v0:
```python
import math

import jax
import jax.numpy as jnp
from jax import lax
from jax.sharding import PartitionSpec as P

D = 8192
KV_HEADS = 8
HD = 128
PLEN = 256
QLEN = 128
SIDE = 2


def rope_tables(positions):
    half_dim = HD // 2
    inverse = jnp.exp(
        jnp.arange(half_dim, dtype=jnp.float32) * (-2.0 * math.log(500000.0) / HD)
    )
    angles = positions.astype(jnp.float32)[:, None] * inverse[None, :]
    return jnp.cos(angles), jnp.sin(angles)


def rotate(matrix, tables):
    cosine, sine_part = tables
    half_dim = matrix.shape[-1] // 2
    first_half = matrix[..., :half_dim]
    second = matrix[..., half_dim:]
    return jnp.concatenate(
        [first_half * cosine - second * sine_part, second * cosine + first_half * sine_part],
        axis=-1,
    )


def attend(turned, key_rows, value_rows, question_len):
    scores = lax.dot_general(
        turned, key_rows, (((1,), (1,)), ((), ())), preferred_element_type=jnp.float32
    )
    key_count = key_rows.shape[0]
    cached = key_count - question_len
    row_pos = jnp.arange(turned.shape[0], dtype=jnp.int32) % question_len
    col_pos = jnp.arange(key_count, dtype=jnp.int32)
    allowed = (col_pos[None, :] < cached) | (col_pos[None, :] - cached <= row_pos[:, None])
    scores = jnp.where(allowed, scores, -1e30)
    row_max = jnp.max(scores, axis=1, keepdims=True)
    weights = jnp.where(allowed, jnp.exp(scores - row_max), 0.0)
    total_weight = jnp.sum(weights, axis=1, keepdims=True)
    blended = jnp.dot(weights.astype(jnp.bfloat16), value_rows, preferred_element_type=jnp.float32)
    return blended / total_weight


def one_request(request_q, request_kv, chosen, offsets, stored):
    question_len = request_q.shape[0]
    head_dim = request_kv.shape[1] // 2
    heads_here = request_q.shape[1] // head_dim
    passage_len = stored.shape[1]
    slot_count = chosen.shape[0]
    q_pos = slot_count * passage_len + jnp.arange(question_len, dtype=jnp.int32)
    q_tables = rope_tables(q_pos)
    turned = rotate(
        jnp.transpose(request_q.reshape(question_len, heads_here, head_dim), (1, 0, 2)), q_tables
    ) * HD ** (-0.5)
    turned = turned.astype(jnp.bfloat16).reshape(heads_here * question_len, head_dim)
    picked = stored[chosen].reshape(slot_count * passage_len, 2 * head_dim)
    p_pos = (offsets[:, None] + jnp.arange(passage_len, dtype=jnp.int32)[None, :]).reshape(
        slot_count * passage_len
    )
    key_rows = jnp.concatenate(
        [
            rotate(picked[:, :head_dim].astype(jnp.float32), rope_tables(p_pos)),
            rotate(request_kv[:, :head_dim].astype(jnp.float32), q_tables),
        ],
        axis=0,
    ).astype(jnp.bfloat16)
    value_rows = jnp.concatenate([picked[:, head_dim:], request_kv[:, head_dim:]], axis=0)
    blended = attend(turned, key_rows, value_rows, question_len)
    return jnp.transpose(blended.reshape(heads_here, question_len, head_dim), (1, 0, 2)).reshape(
        question_len, heads_here * head_dim
    )


def line_perms(n):
    depth = n // SIDE
    across = [(h, h ^ 1) for h in range(n)]
    return depth, across


def hop(value, n, senders, direction):
    perm = [
        (z * SIDE + y, (z + direction) * SIDE + y)
        for z in senders
        if 0 <= z + direction < n // SIDE
        for y in range(SIDE)
    ]
    return lax.ppermute(value, "head", perm)


def pick(index, choices):
    result = choices[0]
    left = [c for c in choices if c is not result]
    while left:
        array = left[0]
        mask = False
        for i, choice in enumerate(choices):
            if choice is array:
                mask = mask | (index == i)
        result = jnp.where(mask, array, result)
        left = [c for c in left if c is not array]
    return result


def table_at(index, values):
    return jnp.asarray(values, jnp.int32)[index]


def orders(depth):
    return [sorted(range(depth), key=lambda d, z=z: (-abs(d - z), d)) for z in range(depth)]


def run(processes):
    results = [None] * len(processes)
    answers = [None] * len(processes)
    live = set(range(len(processes)))
    turn = 0
    while live:
        asked = {}
        for i, (start, process) in enumerate(processes):
            if i not in live or start > turn:
                continue
            try:
                asked[i] = process.send(answers[i])
            except StopIteration as stop:
                results[i] = stop.value
                live.discard(i)
        tied = {i: ([array for array, _ in sends], keeps) for i, (sends, keeps) in asked.items()}
        tied = lax.optimization_barrier(tied)
        for i, (sends, _) in asked.items():
            arrays, keeps = tied[i]
            answers[i] = ([move(array) for array, (_, move) in zip(arrays, sends)], keeps)
        turn += 1
    return results


def small_sum(values, n):
    step = 1
    while step < n:
        perm = [(h, h ^ step) for h in range(n)]
        (came,), (values,) = yield [(values, lambda v, perm=perm: lax.ppermute(v, "head", perm))], [values]
        values = values + came
        step *= 2
    return values


def gather_product(part, weight, n):
    depth, across = line_perms(n)
    features = part.shape[1]
    me = lax.axis_index("head")
    z, y = me // SIDE, me % SIDE
    other = 1 - y
    cross = lambda v: lax.ppermute(v, "head", across)
    order = []
    for zz in range(depth):
        near = []
        for s in range(1, depth):
            if zz - s >= 0:
                near.append((s, True))
            if zz + s < depth:
                near.append((s, False))
        order.append(near)

    def product(total, news):
        for came, owner in news:
            rows = lax.dynamic_slice_in_dim(weight, owner * features, features, 0)
            term = jnp.dot(came, rows, preferred_element_type=jnp.float32)
            total = term if total is None else total + term
        return total

    ups, downs = [part], [part]
    total, news, crossing = None, [(part, me)], (part, z)
    for s in range(1, depth + 1):
        sends = [(crossing[0], cross)]
        if s < depth:
            sends.append((ups[-1], lambda v, s=s: hop(v, n, range(s - 1, depth), 1)))
            sends.append((downs[-1], lambda v, s=s: hop(v, n, range(depth - s + 1), -1)))
        owners = [owner for _, owner in news]
        keeps = [[came for came, _ in news]] + ([] if total is None else [total])
        received, keeps = yield sends, keeps
        total = product(keeps[1] if len(keeps) > 1 else None, list(zip(keeps[0], owners)))
        news = [(received[0], crossing[1] * SIDE + other)]
        if s < depth:
            ups.append(received[1])
            downs.append(received[2])
            slot = [order[zz][s - 1] for zz in range(depth)]
            came = pick(z, [(ups if u else downs)[d] for d, u in slot])
            source = table_at(z, [zz - d if u else zz + d for zz, (d, u) in enumerate(slot)])
            crossing = (came, source)
            news.append((came, source * SIDE + y))
    return product(total, news)


def at_offset(z, depth, slots, offset):
    order = orders(depth)
    chosen = [
        slots[order[zz].index(zz + offset)] if 0 <= zz + offset < depth else None
        for zz in range(depth)
    ]
    known = [c for c in chosen if c is not None]
    return pick(z, [known[0] if c is None else c for c in chosen])


def at_distance(z, depth, slots, k):
    order = orders(depth)
    chosen = []
    for zz in range(depth):
        dest = zz + k if zz + k < depth else zz - k
        chosen.append(slots[order[zz].index(dest)] if 0 <= dest < depth else None)
    known = [c for c in chosen if c is not None]
    return pick(z, [known[0] if c is None else c for c in chosen])


def line_sends(z, n, slots, k, came):
    depth = n // SIDE
    up = lambda v: hop(v, n, range(depth - k), 1)
    down = lambda v: hop(v, n, range(k, depth), -1)
    if 2 * k > depth - 1:
        value = at_distance(z, depth, slots, k)
        for array in came:
            value = value + array.astype(jnp.float32)
        value = value.astype(jnp.bfloat16)
        return [(value, up), (value, down)]
    sends = []
    for i, move in enumerate((up, down)):
        value = at_offset(z, depth, slots, -k if i else k)
        if came:
            value = value + came[i].astype(jnp.float32)
        sends.append((value.astype(jnp.bfloat16), move))
    return sends


def scatter_line_first(block_of, source, n):
    depth, across = line_perms(n)
    me = lax.axis_index("head")
    z, y = me // SIDE, me % SIDE
    order = orders(depth)
    dest = [table_at(z, [order[zz][slot] for zz in range(depth)]) for slot in range(depth)]
    slots, came = [block_of(source, dest[0])], []
    if depth > 2:
        slots.append(block_of(source, dest[1]))
    for k in range(depth - 1, 0, -1):
        received, (source, slots) = yield line_sends(z, n, slots, k, came), [source, slots]
        came = received
        while len(slots) < min(depth, depth - k + 2):
            slots = slots + [block_of(source, dest[len(slots)])]
    total = slots[depth - 1] + came[0].astype(jnp.float32) + came[1].astype(jnp.float32)
    first, second = jnp.split(total, 2, axis=1)
    keep = jnp.where(y == 0, first, second)
    give = jnp.where(y == 0, second, first).astype(jnp.bfloat16)
    received, (keep,) = yield [(give, lambda v: lax.ppermute(v, "head", across))], [keep]
    return keep + received[0].astype(jnp.float32)


def scatter_side_first(block_of, source, n):
    depth, across = line_perms(n)
    me = lax.axis_index("head")
    z, y = me // SIDE, me % SIDE
    order = orders(depth)
    cross = lambda v: lax.ppermute(v, "head", across)
    dest = [
        table_at(z, [order[zz][slot] for zz in range(depth)]) * SIDE for slot in range(depth)
    ]
    slots, came = [], []
    give = block_of(source, dest[0] + 1 - y).astype(jnp.bfloat16)
    for turn in range(depth):
        sends = [(give, cross)]
        if turn:
            sends += line_sends(z, n, slots, depth - turn, came)
        received, (source, slots) = yield sends, [source, slots]
        came = received[1:]
        if turn + 1 < depth:
            give = block_of(source, dest[turn + 1] + 1 - y).astype(jnp.bfloat16)
        mine = block_of(source, dest[turn] + y)
        slots = slots + [mine + received[0].astype(jnp.float32)]
    total = slots[depth - 1]
    for array in came:
        total = total + array.astype(jnp.float32)
    return total


def spread_heads(matrix, group_size):
    if group_size == 1:
        return matrix
    leading = matrix.shape[0]
    per_head = matrix.reshape(leading, KV_HEADS, 2 * HD)
    return jnp.repeat(per_head, group_size, axis=1).reshape(leading, KV_HEADS * group_size * 2 * HD)


def local(
    passage_states,
    question_states,
    norm_gain,
    query_weight,
    kv_weight,
    out_weight,
    passage_ids,
    slot_offsets,
):
    n = lax.axis_size("head")
    pas_rows = passage_states.shape[0]
    question_rows = question_states.shape[0]
    features = norm_gain.shape[0]
    group_size = n // KV_HEADS
    block_cols = kv_weight.shape[1] // n
    query_cols = query_weight.shape[1]

    def normed(states):
        rows = states.astype(jnp.float32)
        return (rows * norm_gain[None, :]).astype(jnp.bfloat16), jnp.sum(rows * rows, axis=1)

    gained_q, squares_q = normed(question_states)
    gained_p, squares_p = normed(passage_states)
    spread = spread_heads(kv_weight, group_size)

    def kv_columns(cols):
        def block_of(rows, index):
            weight = lax.dynamic_slice_in_dim(spread, index * cols, cols, 1)
            return jnp.dot(rows, weight, preferred_element_type=jnp.float32)

        return block_of

    query_sums, squares, passage_sums, request_sums = run(
        [
            (0, gather_product(gained_q, query_weight, n)),
            (1, small_sum(jnp.concatenate([squares_p, squares_q]), n)),
            (1, scatter_line_first(kv_columns(SIDE * 2 * HD), gained_p, n)),
            (1, scatter_side_first(kv_columns(2 * HD), gained_q, n)),
        ]
    )
    row_scale = lax.rsqrt(squares / D + 1e-05)[:, None]
    passage_kv = (row_scale[:pas_rows] * passage_sums).astype(jnp.bfloat16)
    request_kv = (row_scale[pas_rows:] * request_sums).astype(jnp.bfloat16)
    own_start = lax.axis_index("head") % group_size * block_cols
    passage_out = lax.dynamic_slice_in_dim(passage_kv, own_start, block_cols, 1)
    queries = row_scale[pas_rows:] * query_sums

    stored = lax.all_gather(passage_kv, "item", axis=0, tiled=True)
    stored = stored.reshape(stored.shape[0] // PLEN, PLEN, stored.shape[1])
    request_count = question_rows // QLEN
    blended = jax.vmap(one_request, in_axes=(0, 0, 0, 0, None))(
        queries.reshape(request_count, QLEN, query_cols),
        request_kv.reshape(request_count, QLEN, request_kv.shape[1]),
        passage_ids,
        slot_offsets,
        stored,
    )
    attention = blended.reshape(question_rows, query_cols).astype(jnp.bfloat16)

    def out_block(rows, device):
        columns = lax.dynamic_slice_in_dim(out_weight, device * features, features, 1)
        return jnp.dot(rows, columns, preferred_element_type=jnp.float32)

    (summed,) = run([(0, scatter_side_first(out_block, attention, n))])
    question_out = (question_states.astype(jnp.float32) + summed).astype(jnp.bfloat16)
    return (passage_out, question_out)


def solution(mesh):
    return jax.shard_map(
        local,
        mesh=mesh,
        in_specs=(
            P(("grp", "item"), "head"),
            P(("grp", "item"), "head"),
            P("head"),
            P(None, "head"),
            P("head", None),
            P("head", None),
            P(("grp", "item"), None),
            P(("grp", "item"), None),
        ),
        out_specs=(P(("grp", "item"), "head"), P(("grp", "item"), "head")),
        check_vma=False,
    )
```

profile of v0, /device:TPU:0, one launch (start us, length us, event | category | flops | bytes accessed | tf_op | source)
XLA Modules:
  0.0 408.9 jit_solution(8728072051626240041)
XLA Ops:
  8.9 5.0 %collective-permute-start = (bf16[512,1024]{1,0:T(8,128)(2,1)S(1)}, bf16[512,1024]{1,0:T(8,128)(2,1)S(1)}, u32[]{:S(2)}, u32[]{:S(2)}) collective-permute-start(bf16[512,1024]{1,0:T(8,128)(2,1)S(1)} %get-tuple-element.128), channel_id=1, source_target_pairs={{0,4},{2,6},{4,8},{6,10},{8,12},{10,14},{1,5},{3,7},{5,9},{7,11},{... | collective-permute-start | bytes 3145736 | tf_op jit(solution)/shard_map/ppermute | solution.py:96
  28.7 4.9 %fusion.151 = (bf16[1024,512]{1,0:T(8,128)(2,1)}, f32[1024,512]{1,0:T(8,128)}) fusion(bf16[1024,1024]{1,0:T(8,128)(2,1)} %get-tuple-element.106, bf16[1024,2048]{1,0:T(8,128)(2,1)} %param.27, s32[]{:T(128)S(6)} %select_n.239), kind=kOutput, calls=%fused_computation.185 | convolution fusion | flops 1074266112 | bytes 6291460 | tf_op jit(solution)/shard_map/dot_general | solution.py:327
  50.0 8.3 %collective-permute-start.7 = (bf16[1024,512]{1,0:T(8,128)(2,1)S(1)}, bf16[1024,512]{1,0:T(8,128)(2,1)S(1)}, u32[]{:S(2)}, u32[]{:S(2)}) collective-permute-start(bf16[1024,512]{1,0:T(8,128)(2,1)S(1)} %copy-done.17), channel_id=1, source_target_pairs={{0,4},{2,6},{1,5},{3,7},{16,20},{18,22},{17,21},{19,23}} | collective-permute-start | bytes 3145736 | tf_op jit(solution)/shard_map/ppermute | solution.py:96
  79.7 14.1 %collective-permute-done.5 = bf16[512,1024]{1,0:T(8,128)(2,1)} collective-permute-done((bf16[512,1024]{1,0:T(8,128)(2,1)S(1)}, bf16[512,1024]{1,0:T(8,128)(2,1)}, u32[]{:S(2)}, u32[]{:S(2)}) %collective-permute-start.5) | collective-permute-done | bytes 1048608 | tf_op jit(solution)/shard_map/ppermute | solution.py:161
  107.3 10.8 %collective-permute-done.13 = f32[1536]{0:T(1024)S(1)} collective-permute-done((f32[1536]{0:T(1024)S(1)}, f32[1536]{0:T(1024)S(1)}, u32[]{:S(2)}, u32[]{:S(2)}) %collective-permute-start.13) | collective-permute-done | bytes 6176 | tf_op jit(solution)/shard_map/ppermute | solution.py:149
  122.5 4.5 %collective-permute-start.17 = (bf16[512,256]{1,0:T(8,128)(2,1)S(1)}, bf16[512,256]{1,0:T(8,128)(2,1)S(1)}, u32[]{:S(2)}, u32[]{:S(2)}) collective-permute-start(bf16[512,256]{1,0:T(8,128)(2,1)S(1)} %get-tuple-element.110), channel_id=1, source_target_pairs={{0,4},{2,6},{1,5},{3,7},{16,20},{18,22},{17,21},{19,23}} | collective-permute-start | bytes 786440 | tf_op jit(solution)/shard_map/ppermute | solution.py:96
  128.5 16.1 %collective-permute-done.17 = bf16[512,256]{1,0:T(8,128)(2,1)S(1)} collective-permute-done((bf16[512,256]{1,0:T(8,128)(2,1)S(1)}, bf16[512,256]{1,0:T(8,128)(2,1)S(1)}, u32[]{:S(2)}, u32[]{:S(2)}) %collective-permute-start.17) | collective-permute-done | bytes 262176 | tf_op jit(solution)/shard_map/ppermute | solution.py:96
  147.4 16.9 %collective-permute-done.12 = bf16[512,1024]{1,0:T(8,128)(2,1)S(1)} collective-permute-done((bf16[512,1024]{1,0:T(8,128)(2,1)S(1)}, bf16[512,1024]{1,0:T(8,128)(2,1)S(1)}, u32[]{:S(2)}, u32[]{:S(2)}) %collective-permute-start.12) | collective-permute-done | bytes 1048608 | tf_op jit(solution)/shard_map/ppermute | solution.py:161
  165.5 5.1 %collective-permute-start.20 = (bf16[1024,512]{1,0:T(8,128)(2,1)S(1)}, bf16[1024,512]{1,0:T(8,128)(2,1)S(1)}, u32[]{:S(2)}, u32[]{:S(2)}) collective-permute-start(bf16[1024,512]{1,0:T(8,128)(2,1)S(1)} %get-tuple-element.115), channel_id=1, source_target_pairs={{0,4},{2,6},{4,8},{6,10},{8,12},{10,14},{1,5},{3,7},{5,9},{7,11},{... | collective-permute-start | bytes 3145736 | tf_op jit(solution)/shard_map/ppermute | solution.py:96
  173.5 4.6 %collective-permute-start.19 = (f32[1536]{0:T(1024)S(1)}, f32[1536]{0:T(1024)S(1)}, u32[]{:S(2)}, u32[]{:S(2)}) collective-permute-start(f32[1536]{0:T(1024)S(1)} %add.406), channel_id=1, source_target_pairs={{0,8},{2,10},{4,12},{6,14},{8,0},{10,2},{12,4},{14,6},{1,9},{3,11}... | collective-permute-start | bytes 18440 | tf_op jit(solution)/shard_map/ppermute | solution.py:149
  182.8 9.9 %collective-permute-done.19 = f32[1536]{0:T(1024)S(1)} collective-permute-done((f32[1536]{0:T(1024)S(1)}, f32[1536]{0:T(1024)S(1)}, u32[]{:S(2)}, u32[]{:S(2)}) %collective-permute-start.19) | collective-permute-done | bytes 6176 | tf_op jit(solution)/shard_map/ppermute | solution.py:149
  202.4 5.7 %collective-permute-start.28 = (bf16[512,256]{1,0:T(8,128)(2,1)S(1)}, bf16[512,256]{1,0:T(8,128)(2,1)}, u32[]{:S(2)}, u32[]{:S(2)}) collective-permute-start(bf16[512,256]{1,0:T(8,128)(2,1)S(1)} %get-tuple-element.130), channel_id=1, source_target_pairs={{0,4},{2,6},{4,8},{6,10},{8,12},{10,14},{1,5},{3,7},{5,9},{7,11},{... | collective-permute-start | bytes 786440 | tf_op jit(solution)/shard_map/ppermute | solution.py:96
  208.6 11.5 %collective-permute-done.26 = bf16[512,1024]{1,0:T(8,128)(2,1)S(1)} collective-permute-done((bf16[512,1024]{1,0:T(8,128)(2,1)S(1)}, bf16[512,1024]{1,0:T(8,128)(2,1)S(1)}, u32[]{:S(2)}, u32[]{:S(2)}) %collective-permute-start.26) | collective-permute-done | bytes 1048608 | tf_op jit(solution)/shard_map/ppermute | solution.py:161
  236.9 10.5 %fusion.11 = (bf16[4,1024,64]{2,1,0:T(8,128)(2,1)}, bf16[4,1024,64]{2,1,0:T(8,128)(2,1)}) fusion(f32[4,1024,128]{2,1,0:T(8,128)S(1)} %get-tuple-element.155, f32[64]{0:T(128)S(1)} %multiply_exponential_fusion, f32[4,1024]{1,0:T(4,128)S(1)} %copy-done.13), kind=kLoop, calls=%fused_computation.22 | loop fusion | flops 2359296 | bytes 3162368 | tf_op jit(solution)/shard_map/convert.4
  247.5 15.5 %fusion.153 = (f32[4,1024]{1,0:T(4,128)}, bf16[4,1024,1152]{2,1,0:T(8,128)(2,1)}) fusion(pred[1024,1152]{1,0:T(8,128)(4,1)} %compare_or_fusion, bf16[4,128,64]{2,1,0:T(8,128)(2,1)S(1)} %copy-done.12, bf16[4,128,64]{2,1,0:T(8,128)(2,1)S(1)} %get-tuple-element.164, bf16[4,1024,64]{2,1,0:T(8,128)(2,1)} %get-tuple-element.151, ...), kind=kOutput, calls=%fused_computation.187 | convolution fusion | flops 1237845120 | bytes 13910016 | tf_op jit(solution)/shard_map/vmap()/sub | solution.py:47
  263.0 6.3 %divide_convert_fusion = bf16[4,1024,128]{2,1,0:T(8,128)(2,1)S(1)} fusion(f32[4,1024]{1,0:T(4,128)} %get-tuple-element.174, bf16[4,128,128]{2,1,0:T(8,128)(2,1)S(1)} %get-tuple-element.166, bf16[4,1024,128]{2,1,0:T(8,128)(2,1)S(1)} %get-tuple-element.154, bf16[4,1024,1152]{2,1,0:T(8,128)(2,1)} %get-tuple-element.175), kind=kOutput, calls=%fused_computation.53 | convolution fusion | flops 1211367424 | bytes 11681792 | tf_op jit(solution)/shard_map/vmap()/dot_general | solution.py:49
  278.7 19.8 %collective-permute-done.30 = bf16[512,1024]{1,0:T(8,128)(2,1)S(1)} collective-permute-done((bf16[512,1024]{1,0:T(8,128)(2,1)S(1)}, bf16[512,1024]{1,0:T(8,128)(2,1)S(1)}, u32[]{:S(2)}, u32[]{:S(2)}) %collective-permute-start.30) | collective-permute-done | bytes 1048608 | tf_op jit(solution)/shard_map/ppermute | solution.py:268
  298.5 4.5 %fusion.156 = (bf16[512,1024]{1,0:T(8,128)(2,1)}, f32[512,1024]{1,0:T(8,128)}) fusion(bf16[512,1024]{1,0:T(8,128)(2,1)S(1)} %collective-permute-done.30, bf16[512,1024]{1,0:T(8,128)(2,1)S(1)} %bitcast.66, bf16[1024,8192]{1,0:T(8,128)(2,1)} %param.28, s32[]{:T(128)S(6)} %select_n.276), kind=kOutput, calls=%fused_computation.188 | convolution fusion | flops 1075314688 | bytes 7340036 | tf_op jit(solution)/shard_map/dot_general | solution.py:360
  313.3 16.5 %collective-permute-done.32 = bf16[512,1024]{1,0:T(8,128)(2,1)S(1)} collective-permute-done((bf16[512,1024]{1,0:T(8,128)(2,1)}, bf16[512,1024]{1,0:T(8,128)(2,1)S(1)}, u32[]{:S(2)}, u32[]{:S(2)}) %collective-permute-start.32) | collective-permute-done | bytes 1048608 | tf_op jit(solution)/shard_map/ppermute | solution.py:96
  332.3 5.1 %add_convert_fusion.2 = (bf16[512,1024]{1,0:T(8,128)(2,1)}, f32[512,1024]{1,0:T(8,128)S(1)}) fusion(bf16[512,1024]{1,0:T(8,128)(2,1)} %copy-done.9, bf16[512,1024]{1,0:T(8,128)(2,1)} %copy-done.10, f32[512,1024]{1,0:T(8,128)S(1)} %copy-done.8, pred[]{:T(512)S(6)} %or.22, bf16[512,1024]{1,0:T(8,128)(2,1)} %collective-permute-done.31, ...), kind=kOutput, calls=%fused_computation.40 | convolution fusion | flops 1077936128 | bytes 11534341 | tf_op jit(solution)/shard_map/dot_general | solution.py:360
  347.8 13.3 %collective-permute-done.34 = bf16[512,1024]{1,0:T(8,128)(2,1)} collective-permute-done((bf16[512,1024]{1,0:T(8,128)(2,1)}, bf16[512,1024]{1,0:T(8,128)(2,1)}, u32[]{:S(2)}, u32[]{:S(2)}) %collective-permute-start.34) | collective-permute-done | bytes 1048608 | tf_op jit(solution)/shard_map/ppermute | solution.py:268
  369.3 5.0 %collective-permute-start.38 = (bf16[512,1024]{1,0:T(8,128)(2,1)}, bf16[512,1024]{1,0:T(8,128)(2,1)S(1)}, u32[]{:S(2)}, u32[]{:S(2)}) collective-permute-start(bf16[512,1024]{1,0:T(8,128)(2,1)} %get-tuple-element.146), channel_id=1, source_target_pairs={{0,4},{2,6},{4,8},{6,10},{8,12},{10,14},{1,5},{3,7},{5,9},{7,11},{... | collective-permute-start | bytes 3145736 | tf_op jit(solution)/shard_map/ppermute | solution.py:96
  375.5 17.8 %collective-permute-done.39 = bf16[512,1024]{1,0:T(8,128)(2,1)S(1)} collective-permute-done((bf16[512,1024]{1,0:T(8,128)(2,1)}, bf16[512,1024]{1,0:T(8,128)(2,1)S(1)}, u32[]{:S(2)}, u32[]{:S(2)}) %collective-permute-start.39) | collective-permute-done | bytes 1048608 | tf_op jit(solution)/shard_map/ppermute | solution.py:96
  396.9 4.8 %fusion.16 = bf16[512,1024]{1,0:T(8,128)(2,1)} fusion(bf16[512,1024]{1,0:T(8,128)(2,1)} %param.24, bf16[512,1024]{1,0:T(8,128)(2,1)S(1)} %collective-permute-done.39, bf16[512,1024]{1,0:T(8,128)(2,1)S(1)} %collective-permute-done.38, bf16[512,1024]{1,0:T(8,128)(2,1)} %collective-permute-done.37, bf16[512,1024]{1,0:T(8,128)(2,1)S(1)} %bitcast.71, ...), kind=kOutput, calls=%fused_computation.27 | convolution fusion | flops 1078460416 | bytes 8388612 | tf_op jit(solution)/shard_map/dot_general | solution.py:360
  (199 shorter events, 151.5 us)
Async XLA Ops:
  7.3 227.0 %all-gather.2.cloned.1.call-start = ((), (), s32[]{:S(2)}) async-start(), calls=%async_computation | async-start | bytes 1572864 | tf_op jit(solution)/shard_map/all_gather | solution.py:346
  8.9 37.5 %collective-permute-start = (bf16[512,1024]{1,0:T(8,128)(2,1)S(1)}, bf16[512,1024]{1,0:T(8,128)(2,1)S(1)}, u32[]{:S(2)}, u32[]{:S(2)}) collective-permute-start(bf16[512,1024]{1,0:T(8,128)(2,1)S(1)} %get-tuple-element.128), channel_id=1, source_target_pairs={{0,4},{2,6},{4,8},{6,10},{8,12},{10,14},{1,5},{3,7},{5,9},{7,11},{... | collective-permute-start | bytes 3145736 | tf_op jit(solution)/shard_map/ppermute | solution.py:96
  13.9 32.5 %collective-permute-start.1 = (bf16[512,1024]{1,0:T(8,128)(2,1)S(1)}, bf16[512,1024]{1,0:T(8,128)(2,1)S(1)}, u32[]{:S(2)}, u32[]{:S(2)}) collective-permute-start(bf16[512,1024]{1,0:T(8,128)(2,1)S(1)} %get-tuple-element.128), channel_id=1, source_target_pairs={{4,0},{6,2},{8,4},{10,6},{12,8},{14,10},{5,1},{7,3},{9,5},{11,7},{... | collective-permute-start | bytes 3145736 | tf_op jit(solution)/shard_map/ppermute | solution.py:96
  15.2 31.3 %collective-permute-start.2 = (bf16[512,1024]{1,0:T(8,128)(2,1)S(1)}, bf16[512,1024]{1,0:T(8,128)(2,1)}, u32[]{:S(2)}, u32[]{:S(2)}) collective-permute-start(bf16[512,1024]{1,0:T(8,128)(2,1)S(1)} %get-tuple-element.128), channel_id=1, source_target_pairs={{0,2},{2,0},{4,6},{6,4},{8,10},{10,8},{12,14},{14,12},{1,3},{3,1},... | collective-permute-start | bytes 3145736 | tf_op jit(solution)/shard_map/ppermute | solution.py:161
  46.6 27.9 %collective-permute-start.3 = (bf16[512,1024]{1,0:T(8,128)(2,1)S(1)}, bf16[512,1024]{1,0:T(8,128)(2,1)S(1)}, u32[]{:S(2)}, u32[]{:S(2)}) collective-permute-start(bf16[512,1024]{1,0:T(8,128)(2,1)S(1)} %collective-permute-done), channel_id=1, source_target_pairs={{4,8},{6,10},{8,12},{10,14},{5,9},{7,11},{9,13},{11,15},{20,24},{2... | collective-permute-start | bytes 3145736 | tf_op jit(solution)/shard_map/ppermute | solution.py:96
  47.4 29.3 %collective-permute-start.4 = (bf16[512,1024]{1,0:T(8,128)(2,1)S(1)}, bf16[512,1024]{1,0:T(8,128)(2,1)S(1)}, u32[]{:S(2)}, u32[]{:S(2)}) collective-permute-start(bf16[512,1024]{1,0:T(8,128)(2,1)S(1)} %collective-permute-done.1), channel_id=1, source_target_pairs={{4,0},{6,2},{8,4},{10,6},{5,1},{7,3},{9,5},{11,7},{20,16},{22,18},... | collective-permute-start | bytes 3145736 | tf_op jit(solution)/shard_map/ppermute | solution.py:96
  49.3 27.6 %collective-permute-start.8 = (bf16[1024,512]{1,0:T(8,128)(2,1)S(1)}, bf16[1024,512]{1,0:T(8,128)(2,1)S(1)}, u32[]{:S(2)}, u32[]{:S(2)}) collective-permute-start(bf16[1024,512]{1,0:T(8,128)(2,1)S(1)} %copy-done.17), channel_id=1, source_target_pairs={{12,8},{14,10},{13,9},{15,11},{28,24},{30,26},{29,25},{31,27}} | collective-permute-start | bytes 3145736 | tf_op jit(solution)/shard_map/ppermute | solution.py:96
  50.0 28.9 %collective-permute-start.7 = (bf16[1024,512]{1,0:T(8,128)(2,1)S(1)}, bf16[1024,512]{1,0:T(8,128)(2,1)S(1)}, u32[]{:S(2)}, u32[]{:S(2)}) collective-permute-start(bf16[1024,512]{1,0:T(8,128)(2,1)S(1)} %copy-done.17), channel_id=1, source_target_pairs={{0,4},{2,6},{1,5},{3,7},{16,20},{18,22},{17,21},{19,23}} | collective-permute-start | bytes 3145736 | tf_op jit(solution)/shard_map/ppermute | solution.py:96
  93.8 52.4 %collective-permute-start.10 = (bf16[512,1024]{1,0:T(8,128)(2,1)S(1)}, bf16[512,1024]{1,0:T(8,128)(2,1)S(1)}, u32[]{:S(2)}, u32[]{:S(2)}) collective-permute-start(bf16[512,1024]{1,0:T(8,128)(2,1)S(1)} %collective-permute-done.3), channel_id=1, source_target_pairs={{8,12},{10,14},{9,13},{11,15},{24,28},{26,30},{25,29},{27,31}} | collective-permute-start | bytes 3145736 | tf_op jit(solution)/shard_map/ppermute | solution.py:96
  94.6 51.7 %collective-permute-start.11 = (bf16[512,1024]{1,0:T(8,128)(2,1)S(1)}, bf16[512,1024]{1,0:T(8,128)(2,1)S(1)}, u32[]{:S(2)}, u32[]{:S(2)}) collective-permute-start(bf16[512,1024]{1,0:T(8,128)(2,1)S(1)} %collective-permute-done.4), channel_id=1, source_target_pairs={{4,0},{6,2},{5,1},{7,3},{20,16},{22,18},{21,17},{23,19}} | collective-permute-start | bytes 3145736 | tf_op jit(solution)/shard_map/ppermute | solution.py:96
  118.1 28.4 %collective-permute-start.15 = (bf16[1024,512]{1,0:T(8,128)(2,1)S(1)}, bf16[1024,512]{1,0:T(8,128)(2,1)S(1)}, u32[]{:S(2)}, u32[]{:S(2)}) collective-permute-start(bf16[1024,512]{1,0:T(8,128)(2,1)S(1)} %add_convert_fusion.5), channel_id=1, source_target_pairs={{8,4},{10,6},{12,8},{14,10},{9,5},{11,7},{13,9},{15,11},{24,20},{2... | collective-permute-start | bytes 3145736 | tf_op jit(solution)/shard_map/ppermute | solution.py:96
  118.9 27.7 %collective-permute-start.14 = (bf16[1024,512]{1,0:T(8,128)(2,1)S(1)}, bf16[1024,512]{1,0:T(8,128)(2,1)S(1)}, u32[]{:S(2)}, u32[]{:S(2)}) collective-permute-start(bf16[1024,512]{1,0:T(8,128)(2,1)S(1)} %add_convert_fusion.5), channel_id=1, source_target_pairs={{0,4},{2,6},{4,8},{6,10},{1,5},{3,7},{5,9},{7,11},{16,20},{18,22},... | collective-permute-start | bytes 3145736 | tf_op jit(solution)/shard_map/ppermute | solution.py:96
  164.3 34.5 %collective-permute-start.21 = (bf16[1024,512]{1,0:T(8,128)(2,1)S(1)}, bf16[1024,512]{1,0:T(8,128)(2,1)S(1)}, u32[]{:S(2)}, u32[]{:S(2)}) collective-permute-start(bf16[1024,512]{1,0:T(8,128)(2,1)S(1)} %get-tuple-element.116), channel_id=1, source_target_pairs={{4,0},{6,2},{8,4},{10,6},{12,8},{14,10},{5,1},{7,3},{9,5},{11,7},{... | collective-permute-start | bytes 3145736 | tf_op jit(solution)/shard_map/ppermute | solution.py:96
  165.5 33.2 %collective-permute-start.20 = (bf16[1024,512]{1,0:T(8,128)(2,1)S(1)}, bf16[1024,512]{1,0:T(8,128)(2,1)S(1)}, u32[]{:S(2)}, u32[]{:S(2)}) collective-permute-start(bf16[1024,512]{1,0:T(8,128)(2,1)S(1)} %get-tuple-element.115), channel_id=1, source_target_pairs={{0,4},{2,6},{4,8},{6,10},{8,12},{10,14},{1,5},{3,7},{5,9},{7,11},{... | collective-permute-start | bytes 3145736 | tf_op jit(solution)/shard_map/ppermute | solution.py:96
  170.6 26.6 %collective-permute-start.24 = (bf16[512,256]{1,0:T(8,128)(2,1)S(1)}, bf16[512,256]{1,0:T(8,128)(2,1)S(1)}, u32[]{:S(2)}, u32[]{:S(2)}) collective-permute-start(bf16[512,256]{1,0:T(8,128)(2,1)S(1)} %add_convert_fusion.8), channel_id=1, source_target_pairs={{8,4},{10,6},{12,8},{14,10},{9,5},{11,7},{13,9},{15,11},{24,20},{2... | collective-permute-start | bytes 786440 | tf_op jit(solution)/shard_map/ppermute | solution.py:96
  194.1 26.0 %collective-permute-start.26 = (bf16[512,1024]{1,0:T(8,128)(2,1)S(1)}, bf16[512,1024]{1,0:T(8,128)(2,1)S(1)}, u32[]{:S(2)}, u32[]{:S(2)}) collective-permute-start(bf16[512,1024]{1,0:T(8,128)(2,1)S(1)} %select_select_fusion), channel_id=1, source_target_pairs={{0,2},{2,0},{4,6},{6,4},{8,10},{10,8},{12,14},{14,12},{1,3},{3,1},... | collective-permute-start | bytes 3145736 | tf_op jit(solution)/shard_map/ppermute | solution.py:161
  199.5 26.2 %collective-permute-start.25 = (bf16[1024,256]{1,0:T(8,128)(2,1)S(1)}, bf16[1024,256]{1,0:T(8,128)(2,1)S(1)}, u32[]{:S(2)}, u32[]{:S(2)}) collective-permute-start(bf16[1024,256]{1,0:T(8,128)(2,1)S(1)} %select_convert_fusion), channel_id=1, source_target_pairs={{0,2},{2,0},{4,6},{6,4},{8,10},{10,8},{12,14},{14,12},{1,3},{3,1},... | collective-permute-start | bytes 1572872 | tf_op jit(solution)/shard_map/ppermute | solution.py:259
  201.1 30.0 %collective-permute-start.29 = (bf16[512,256]{1,0:T(8,128)(2,1)}, bf16[512,256]{1,0:T(8,128)(2,1)}, u32[]{:S(2)}, u32[]{:S(2)}) collective-permute-start(bf16[512,256]{1,0:T(8,128)(2,1)} %get-tuple-element.131), channel_id=1, source_target_pairs={{4,0},{6,2},{8,4},{10,6},{12,8},{14,10},{5,1},{7,3},{9,5},{11,7},{... | collective-permute-start | bytes 786440 | tf_op jit(solution)/shard_map/ppermute | solution.py:96
  202.4 28.7 %collective-permute-start.28 = (bf16[512,256]{1,0:T(8,128)(2,1)S(1)}, bf16[512,256]{1,0:T(8,128)(2,1)}, u32[]{:S(2)}, u32[]{:S(2)}) collective-permute-start(bf16[512,256]{1,0:T(8,128)(2,1)S(1)} %get-tuple-element.130), channel_id=1, source_target_pairs={{0,4},{2,6},{4,8},{6,10},{8,12},{10,14},{1,5},{3,7},{5,9},{7,11},{... | collective-permute-start | bytes 786440 | tf_op jit(solution)/shard_map/ppermute | solution.py:96
  273.1 25.4 %collective-permute-start.30 = (bf16[512,1024]{1,0:T(8,128)(2,1)S(1)}, bf16[512,1024]{1,0:T(8,128)(2,1)S(1)}, u32[]{:S(2)}, u32[]{:S(2)}) collective-permute-start(bf16[512,1024]{1,0:T(8,128)(2,1)S(1)} %fusion.54), channel_id=1, source_target_pairs={{0,2},{2,0},{4,6},{6,4},{8,10},{10,8},{12,14},{14,12},{1,3},{3,1},... | collective-permute-start | bytes 3145736 | tf_op jit(solution)/shard_map/ppermute | solution.py:268
  303.7 26.0 %collective-permute-start.32 = (bf16[512,1024]{1,0:T(8,128)(2,1)}, bf16[512,1024]{1,0:T(8,128)(2,1)S(1)}, u32[]{:S(2)}, u32[]{:S(2)}) collective-permute-start(bf16[512,1024]{1,0:T(8,128)(2,1)} %get-tuple-element.137), channel_id=1, source_target_pairs={{0,4},{2,6},{1,5},{3,7},{16,20},{18,22},{17,21},{19,23}} | collective-permute-start | bytes 3145736 | tf_op jit(solution)/shard_map/ppermute | solution.py:96
  338.9 25.3 %collective-permute-start.36 = (bf16[512,1024]{1,0:T(8,128)(2,1)}, bf16[512,1024]{1,0:T(8,128)(2,1)}, u32[]{:S(2)}, u32[]{:S(2)}) collective-permute-start(bf16[512,1024]{1,0:T(8,128)(2,1)} %get-tuple-element.141), channel_id=1, source_target_pairs={{8,4},{10,6},{12,8},{14,10},{9,5},{11,7},{13,9},{15,11},{24,20},{2... | collective-permute-start | bytes 3145736 | tf_op jit(solution)/shard_map/ppermute | solution.py:96
  368.0 25.3 %collective-permute-start.39 = (bf16[512,1024]{1,0:T(8,128)(2,1)}, bf16[512,1024]{1,0:T(8,128)(2,1)S(1)}, u32[]{:S(2)}, u32[]{:S(2)}) collective-permute-start(bf16[512,1024]{1,0:T(8,128)(2,1)} %get-tuple-element.147), channel_id=1, source_target_pairs={{4,0},{6,2},{8,4},{10,6},{12,8},{14,10},{5,1},{7,3},{9,5},{11,7},{... | collective-permute-start | bytes 3145736 | tf_op jit(solution)/shard_map/ppermute | solution.py:96
  369.3 25.3 %collective-permute-start.38 = (bf16[512,1024]{1,0:T(8,128)(2,1)}, bf16[512,1024]{1,0:T(8,128)(2,1)S(1)}, u32[]{:S(2)}, u32[]{:S(2)}) collective-permute-start(bf16[512,1024]{1,0:T(8,128)(2,1)} %get-tuple-element.146), channel_id=1, source_target_pairs={{0,4},{2,6},{4,8},{6,10},{8,12},{10,14},{1,5},{3,7},{5,9},{7,11},{... | collective-permute-start | bytes 3145736 | tf_op jit(solution)/shard_map/ppermute | solution.py:96
  (46 other events, 732.5 us)
Sparse Core Ops, SparseCore 0:
  226.9 7.3 all-gather.1
where the time goes:
time: 416 us; the launch traced here: 409 us
  waiting for transfers between devices  165 us (40%)
  matrix products  96.6 us (23%)
  starting transfers between devices  86.3 us (21%)
  other arithmetic  29 us (7%)
  between operations  20.5 us (5%)
  local copies, waits for them, and re-layouts  11.5 us (3%)
    ppermute x24, starting transfers between devices, hop(): return lax.ppermute(value, 'head', perm)  59.2 us
    ppermute x24, waiting for transfers between devices, hop(): return lax.ppermute(value, 'head', perm)  56.8 us
    ppermute x4, waiting for transfers between devices, gather_product(): cross = lambda v: lax.ppermute(v, 'head', across)  42.6 us
    ppermute x8, waiting for transfers between devices, scatter_side_first(): cross = lambda v: lax.ppermute(v, 'head', across)  40.7 us
    dot_general x8, matrix products, out_block(): return jnp.dot(rows, columns, preferred_element_type=jnp.float32)  32.2 us
    dot_general x12, matrix products, block_of(): return jnp.dot(rows, weight, preferred_element_type=jnp.float32)  24.1 us
    ppermute x3, waiting for transfers between devices, small_sum(): lax.ppermute(v, 'head', perm)  20.8 us
    dot_general x8, matrix products, product(): term = jnp.dot(came, rows, preferred_element_type=jnp.float32)  18.6 us
  transfers between devices with their start and end apart: 41, of which 19 were waited for; matrix products, arithmetic and copies ran while one was open for 19% of the time, Pallas kernels for 0%

commit v1 on v0

--- a/solution.py
+++ b/solution.py
@@ -118,85 +118,30 @@
     return [sorted(range(depth), key=lambda d, z=z: (-abs(d - z), d)) for z in range(depth)]
 
 
-def run(processes):
-    results = [None] * len(processes)
-    answers = [None] * len(processes)
-    live = set(range(len(processes)))
-    turn = 0
-    while live:
-        asked = {}
-        for i, (start, process) in enumerate(processes):
-            if i not in live or start > turn:
-                continue
-            try:
-                asked[i] = process.send(answers[i])
-            except StopIteration as stop:
-                results[i] = stop.value
-                live.discard(i)
-        tied = {i: ([array for array, _ in sends], keeps) for i, (sends, keeps) in asked.items()}
-        tied = lax.optimization_barrier(tied)
-        for i, (sends, _) in asked.items():
-            arrays, keeps = tied[i]
-            answers[i] = ([move(array) for array, (_, move) in zip(arrays, sends)], keeps)
-        turn += 1
-    return results
-
-
-def small_sum(values, n):
-    step = 1
-    while step < n:
-        perm = [(h, h ^ step) for h in range(n)]
-        (came,), (values,) = yield [(values, lambda v, perm=perm: lax.ppermute(v, "head", perm))], [values]
-        values = values + came
-        step *= 2
-    return values
-
-
-def gather_product(part, weight, n):
-    depth, across = line_perms(n)
-    features = part.shape[1]
-    me = lax.axis_index("head")
-    z, y = me // SIDE, me % SIDE
-    other = 1 - y
-    cross = lambda v: lax.ppermute(v, "head", across)
-    order = []
-    for zz in range(depth):
-        near = []
-        for s in range(1, depth):
-            if zz - s >= 0:
-                near.append((s, True))
-            if zz + s < depth:
-                near.append((s, False))
-        order.append(near)
-
-    def product(total, news):
-        for came, owner in news:
-            rows = lax.dynamic_slice_in_dim(weight, owner * features, features, 0)
-            term = jnp.dot(came, rows, preferred_element_type=jnp.float32)
-            total = term if total is None else total + term
-        return total
-
-    ups, downs = [part], [part]
-    total, news, crossing = None, [(part, me)], (part, z)
-    for s in range(1, depth + 1):
-        sends = [(crossing[0], cross)]
-        if s < depth:
-            sends.append((ups[-1], lambda v, s=s: hop(v, n, range(s - 1, depth), 1)))
-            sends.append((downs[-1], lambda v, s=s: hop(v, n, range(depth - s + 1), -1)))
-        owners = [owner for _, owner in news]
-        keeps = [[came for came, _ in news]] + ([] if total is None else [total])
-        received, keeps = yield sends, keeps
-        total = product(keeps[1] if len(keeps) > 1 else None, list(zip(keeps[0], owners)))
-        news = [(received[0], crossing[1] * SIDE + other)]
-        if s < depth:
-            ups.append(received[1])
-            downs.append(received[2])
-            slot = [order[zz][s - 1] for zz in range(depth)]
-            came = pick(z, [(ups if u else downs)[d] for d, u in slot])
-            source = table_at(z, [zz - d if u else zz + d for zz, (d, u) in enumerate(slot)])
-            crossing = (came, source)
-            news.append((came, source * SIDE + y))
-    return product(total, news)
+def tie(*trees):
+    return lax.optimization_barrier(trees)
+
+
+def fold(rows, height):
+    if rows.shape[0] == height:
+        return rows
+    return jnp.concatenate(jnp.split(rows, rows.shape[0] // height, axis=0), axis=1)
+
+
+def unfold(block, cols):
+    if block.shape[1] == cols:
+        return block
+    return jnp.concatenate(jnp.split(block, block.shape[1] // cols, axis=1), axis=0)
+
+
+def widen(array, cols):
+    if array.shape[1] == cols:
+        return array
+    return jnp.pad(array, ((0, 0), (0, cols - array.shape[1])))
+
+
+def join(arrays):
+    return arrays[0] if len(arrays) == 1 else jnp.concatenate(arrays, axis=1)
 
 
 def at_offset(z, depth, slots, offset):
@@ -219,67 +164,169 @@
     return pick(z, [known[0] if c is None else c for c in chosen])
 
 
-def line_sends(z, n, slots, k, came):
+def line_values(z, n, slots, k, came):
     depth = n // SIDE
-    up = lambda v: hop(v, n, range(depth - k), 1)
-    down = lambda v: hop(v, n, range(k, depth), -1)
     if 2 * k > depth - 1:
         value = at_distance(z, depth, slots, k)
-        for array in came:
-            value = value + array.astype(jnp.float32)
+        if came:
+            value = value + jnp.where(z < depth - k, *came).astype(jnp.float32)
         value = value.astype(jnp.bfloat16)
-        return [(value, up), (value, down)]
-    sends = []
-    for i, move in enumerate((up, down)):
+        return value, value
+    values = []
+    for i in range(2):
         value = at_offset(z, depth, slots, -k if i else k)
         if came:
             value = value + came[i].astype(jnp.float32)
-        sends.append((value.astype(jnp.bfloat16), move))
-    return sends
-
-
-def scatter_line_first(block_of, source, n):
+        values.append(value.astype(jnp.bfloat16))
+    return tuple(values)
+
+
+def project(part, passages, query_weight, kv_weight, n):
+    depth, across = line_perms(n)
+    features = part.shape[1]
+    height = part.shape[0]
+    cols = 2 * HD
+    me = lax.axis_index("head")
+    z, y = me // SIDE, me % SIDE
+    other = 1 - y
+    order = orders(depth)
+    dest = [table_at(z, [order[zz][slot] for zz in range(depth)]) for slot in range(depth)]
+    width = max(features, passages.shape[0] // height * SIDE * cols)
+    arrivals = []
+    for zz in range(depth):
+        near = []
+        for s in range(1, depth):
+            if zz - s >= 0:
+                near.append((s, True))
+            if zz + s < depth:
+                near.append((s, False))
+        arrivals.append(near)
+
+    def product(total, news):
+        for came, owner in news:
+            rows = lax.dynamic_slice_in_dim(query_weight, owner * features, features, 0)
+            term = jnp.dot(came, rows, preferred_element_type=jnp.float32)
+            total = term if total is None else total + term
+        return total
+
+    def kv_product(rows, start, count):
+        weight = lax.dynamic_slice_in_dim(kv_weight, start, count, 1)
+        return jnp.dot(rows, weight, preferred_element_type=jnp.float32)
+
+    ups, downs, crossing = [part], [part], (part, z)
+    total, news = None, [(part, me)]
+    p_slots, p_came = [], ()
+    q_slots, q_came, q_give = [], (), None
+    questions = part
+    for t in range(1, depth + 2):
+        to_y = []
+        to_z = ([], [])
+        if t <= depth:
+            to_y.append(crossing[0])
+        if t == 1:
+            for side in to_z:
+                side.append(widen(part, width))
+        elif t <= depth:
+            values = line_values(z, n, p_slots, depth - t + 1, p_came)
+            gathered = (ups[-1], downs[-1])
+            for i, place in enumerate((z, depth - 1 - z)):
+                mine = widen(fold(values[i], height), width)
+                to_z[i].append(jnp.where(place < t - 1, mine, widen(gathered[i], width)))
+        else:
+            p_total = p_slots[depth - 1]
+            for array in p_came:
+                p_total = p_total + array.astype(jnp.float32)
+            first, second = jnp.split(p_total, 2, axis=1)
+            p_keep = jnp.where(y == 0, first, second)
+            to_y.append(fold(jnp.where(y == 0, second, first).astype(jnp.bfloat16), height))
+        if t >= 2:
+            to_y.append(q_give)
+        if t >= 3:
+            for side, value in zip(to_z, line_values(z, n, q_slots, depth - t + 2, q_came)):
+                side.append(value)
+        sends, news_arrays, total, passages, questions, p_slots, q_slots = tie(
+            [join(to_y), join(to_z[0]), join(to_z[1])],
+            [came for came, _ in news],
+            [] if total is None else [total],
+            passages,
+            questions,
+            p_slots,
+            q_slots,
+        )
+        last = t > depth
+        received = [
+            lax.ppermute(sends[0], "head", across),
+            hop(sends[1], n, range(depth), 1),
+            hop(sends[2], n, range(depth), -1),
+        ]
+        total = product(total[0] if total else None, [(c, o) for c, (_, o) in zip(news_arrays, news)])
+        new_p = [kv_product(passages, dest[t - 1] * SIDE * cols, SIDE * cols)] if t <= depth else []
+        q_mine = []
+        if t >= 2:
+            q_mine = [kv_product(questions, (dest[t - 2] * SIDE + y) * cols, cols)]
+        new_give = []
+        if t <= depth:
+            new_give = [
+                kv_product(questions, (dest[t - 1] * SIDE + other) * cols, cols).astype(jnp.bfloat16)
+            ]
+        received, total, new_p, q_mine, new_give = tie(received, total, new_p, q_mine, new_give)
+        p_slots = p_slots + new_p
+        q_give = new_give[0] if new_give else None
+        taken = 0
+        news = []
+        if t <= depth:
+            news.append((received[0][:, :features], crossing[1] * SIDE + other))
+            taken = features
+        else:
+            taken = passages.shape[0] // height * cols
+            p_came_y = unfold(received[0][:, :taken], cols)
+        if t >= 2:
+            q_slots = q_slots + [q_mine[0] + received[0][:, taken:].astype(jnp.float32)]
+        if t < depth:
+            ups.append(received[1][:, :features])
+            downs.append(received[2][:, :features])
+            slot = [arrivals[zz][t - 1] for zz in range(depth)]
+            came = pick(z, [(ups if u else downs)[d] for d, u in slot])
+            source = table_at(z, [zz - d if u else zz + d for zz, (d, u) in enumerate(slot)])
+            crossing = (came, source)
+            news.append((came, source * SIDE + y))
+        if 2 <= t <= depth:
+            used = passages.shape[0] // height * SIDE * cols
+            p_came = tuple(unfold(r[:, :used], SIDE * cols) for r in received[1:])
+        if t >= 3:
+            q_came = tuple(r[:, (0 if last else width) :] for r in received[1:])
+    q_total = q_slots[depth - 1]
+    for array in q_came:
+        q_total = q_total + array.astype(jnp.float32)
+    return product(total, news), p_keep + p_came_y.astype(jnp.float32), q_total
+
+
+def scatter_sum(block_of, source, n):
     depth, across = line_perms(n)
     me = lax.axis_index("head")
     z, y = me // SIDE, me % SIDE
     order = orders(depth)
-    dest = [table_at(z, [order[zz][slot] for zz in range(depth)]) for slot in range(depth)]
-    slots, came = [block_of(source, dest[0])], []
-    if depth > 2:
-        slots.append(block_of(source, dest[1]))
-    for k in range(depth - 1, 0, -1):
-        received, (source, slots) = yield line_sends(z, n, slots, k, came), [source, slots]
-        came = received
-        while len(slots) < min(depth, depth - k + 2):
-            slots = slots + [block_of(source, dest[len(slots)])]
-    total = slots[depth - 1] + came[0].astype(jnp.float32) + came[1].astype(jnp.float32)
-    first, second = jnp.split(total, 2, axis=1)
-    keep = jnp.where(y == 0, first, second)
-    give = jnp.where(y == 0, second, first).astype(jnp.bfloat16)
-    received, (keep,) = yield [(give, lambda v: lax.ppermute(v, "head", across))], [keep]
-    return keep + received[0].astype(jnp.float32)
-
-
-def scatter_side_first(block_of, source, n):
-    depth, across = line_perms(n)
-    me = lax.axis_index("head")
-    z, y = me // SIDE, me % SIDE
-    order = orders(depth)
-    cross = lambda v: lax.ppermute(v, "head", across)
     dest = [
         table_at(z, [order[zz][slot] for zz in range(depth)]) * SIDE for slot in range(depth)
     ]
     slots, came = [], []
     give = block_of(source, dest[0] + 1 - y).astype(jnp.bfloat16)
     for turn in range(depth):
-        sends = [(give, cross)]
+        sends = [give]
         if turn:
-            sends += line_sends(z, n, slots, depth - turn, came)
-        received, (source, slots) = yield sends, [source, slots]
+            sends += line_values(z, n, slots, depth - turn, came)
+        sends, source, slots = tie(sends, source, slots)
+        received = [lax.ppermute(sends[0], "head", across)]
+        if turn:
+            received.append(hop(sends[1], n, range(turn), 1))
+            received.append(hop(sends[2], n, range(depth - turn, depth), -1))
+        mine = block_of(source, dest[turn] + y)
+        gives = []
+        if turn + 1 < depth:
+            gives = [block_of(source, dest[turn + 1] + 1 - y).astype(jnp.bfloat16)]
+        received, mine, gives = tie(received, mine, gives)
+        give = gives[0] if gives else None
         came = received[1:]
-        if turn + 1 < depth:
-            give = block_of(source, dest[turn + 1] + 1 - y).astype(jnp.bfloat16)
-        mine = block_of(source, dest[turn] + y)
         slots = slots + [mine + received[0].astype(jnp.float32)]
     total = slots[depth - 1]
     for array in came:
@@ -321,21 +368,9 @@
     gained_p, squares_p = normed(passage_states)
     spread = spread_heads(kv_weight, group_size)
 
-    def kv_columns(cols):
-        def block_of(rows, index):
-            weight = lax.dynamic_slice_in_dim(spread, index * cols, cols, 1)
-            return jnp.dot(rows, weight, preferred_element_type=jnp.float32)
-
-        return block_of
-
-    query_sums, squares, passage_sums, request_sums = run(
-        [
-            (0, gather_product(gained_q, query_weight, n)),
-            (1, small_sum(jnp.concatenate([squares_p, squares_q]), n)),
-            (1, scatter_line_first(kv_columns(SIDE * 2 * HD), gained_p, n)),
-            (1, scatter_side_first(kv_columns(2 * HD), gained_q, n)),
-        ]
-    )
+    squares = jnp.concatenate([squares_p, squares_q])
+    squares = jnp.sum(lax.all_gather(squares, "head"), axis=0)
+    query_sums, passage_sums, request_sums = project(gained_q, gained_p, query_weight, spread, n)
     row_scale = lax.rsqrt(squares / D + 1e-05)[:, None]
     passage_kv = (row_scale[:pas_rows] * passage_sums).astype(jnp.bfloat16)
     request_kv = (row_scale[pas_rows:] * request_sums).astype(jnp.bfloat16)
@@ -359,7 +394,7 @@
         columns = lax.dynamic_slice_in_dim(out_weight, device * features, features, 1)
         return jnp.dot(rows, columns, preferred_element_type=jnp.float32)
 
-    (summed,) = run([(0, scatter_side_first(out_block, attention, n))])
+    summed = scatter_sum(out_block, attention, n)
     question_out = (question_states.astype(jnp.float32) + summed).astype(jnp.bfloat16)
     return (passage_out, question_out)
 

time: 416 us -> 385 us (0.925)
  waiting for transfers between devices: 165 us -> 93.8 us
  blocking collectives: 0 us -> 49.3 us
  starting transfers between devices: 86.3 us -> 55.8 us
  other arithmetic: 29 us -> 47.4 us
  local copies, waits for them, and re-layouts: 11.5 us -> 21.4 us
  matrix products: 96.6 us -> 89.7 us
    all_gather x0 -> x1, blocking collectives: none -> 49.3 us  [local(): squares = jnp.sum(lax.all_gather(squares, 'head'), axis=0)]
    ppermute x16 -> x9, waiting for transfers between devices: 108 us -> 62.8 us  [the longest x4 42.8 us: scatter_sum(): received = [lax.ppermute(sends[0], 'head', across)]]
    ppermute x24 -> x16, waiting for transfers between devices: 56.8 us -> 31 us  [hop(): return lax.ppermute(value, 'head', perm)]
    ppermute x24 -> x16, starting transfers between devices: 59.2 us -> 43.6 us  [hop(): return lax.ppermute(value, 'head', perm)]
    ppermute x16 -> x9, starting transfers between devices: 27.1 us -> 12.2 us  [the longest x5 6.85 us: project(): lax.ppermute(sends[0], 'head', across)]
    convert_element_type x7 -> x14, other arithmetic: 9.81 us -> 18.1 us  [the longest x5 8.79 us: line_values(): values.append(value.astype(jnp.bfloat16))]
    dot_general x8, matrix products: 32.2 us -> 27.1 us  [out_block(): return jnp.dot(rows, columns, preferred_element_type=jnp.float32)]
    unnamed x62 -> x71, local copies, waits for them, and re-layouts: 2.33 us -> 6.67 us
  transfers between devices with their start and end apart: 41 -> 26, of which waited for: 19 -> 15; matrix products, arithmetic and copies ran while one was open for 19% -> 22% of each run, Pallas kernels for 0% -> 0%
where the time goes in v1:
time: 385 us; the launch traced here: 378 us
  waiting for transfers between devices  93.8 us (24%)
  matrix products  89.7 us (23%)
  starting transfers between devices  55.8 us (14%)
  blocking collectives  49.3 us (13%)
  other arithmetic  47.4 us (12%)
  local copies, waits for them, and re-layouts  21.4 us (6%)
  between operations  20.6 us (5%)
    all_gather x1, blocking collectives, local(): squares = jnp.sum(lax.all_gather(squares, 'head'), axis=0)  49.3 us
    ppermute x16, starting transfers between devices, hop(): return lax.ppermute(value, 'head', perm)  43.6 us
    ppermute x4, waiting for transfers between devices, scatter_sum(): received = [lax.ppermute(sends[0], 'head', across)]  42.8 us
    ppermute x16, waiting for transfers between devices, hop(): return lax.ppermute(value, 'head', perm)  31 us
    dot_general x8, matrix products, out_block(): return jnp.dot(rows, columns, preferred_element_type=jnp.float32)  27.1 us
    dot_general x12, matrix products, kv_product(): return jnp.dot(rows, weight, preferred_element_type=jnp.float32)  21.2 us
    dot_general x8, matrix products, product(): term = jnp.dot(came, rows, preferred_element_type=jnp.float32)  20.4 us
    ppermute x5, waiting for transfers between devices, project(): lax.ppermute(sends[0], 'head', across)  20 us
  transfers between devices with their start and end apart: 26, of which 15 were waited for; matrix products, arithmetic and copies ran while one was open for 22% of the time, Pallas kernels for 0%

profile of v1, /device:TPU:0, one launch (start us, length us, event | category | flops | bytes accessed | tf_op | source)
XLA Modules:
  0.0 377.9 jit_solution(8577296160364434076)
XLA Ops:
  20.2 49.3 %all-gather.1 = f32[8,1,1536]{2,1,0:T(1,128)S(1)} all-gather(f32[1,1,1536]{2,1,0:T(1,128)S(1)} %reshape.246), channel_id=2, replica_groups=mesh['grp'=2,'head'=8,'item'=2] {'head'}, dimensions={0}, use_global_device_ids=true | all-gather | bytes 55296 | tf_op jit(solution)/shard_map/all_gather | solution.py:372
  70.6 4.2 %fusion.48 = f32[512,1024]{1,0:T(8,128)} fusion(bf16[512,1024]{1,0:T(8,128)(2,1)S(1)} %get-tuple-element.173, bf16[8192,1024]{1,0:T(8,128)(2,1)} %param.22, s32[]{:T(128)S(6)} %select_n.284), kind=kOutput, calls=%fused_computation.78 | convolution fusion | flops 1073741824 | bytes 5242884 | tf_op jit(solution)/shard_map/dot_general | solution.py:208
  104.2 5.4 %collective-permute-done.4 = bf16[512,1024]{1,0:T(8,128)(2,1)S(1)} collective-permute-done((bf16[512,1024]{1,0:T(8,128)(2,1)S(1)}, bf16[512,1024]{1,0:T(8,128)(2,1)S(1)}, u32[]{:S(2)}, u32[]{:S(2)}) %collective-permute-start.4) | collective-permute-done | bytes 1048608 | tf_op jit(solution)/shard_map/ppermute | solution.py:96
  109.6 4.4 %collective-permute-done.5 = bf16[512,1024]{1,0:T(8,128)(2,1)S(1)} collective-permute-done((bf16[512,1024]{1,0:T(8,128)(2,1)S(1)}, bf16[512,1024]{1,0:T(8,128)(2,1)S(1)}, u32[]{:S(2)}, u32[]{:S(2)}) %collective-permute-start.5) | collective-permute-done | bytes 1048608 | tf_op jit(solution)/shard_map/ppermute | solution.py:96
  129.2 3.8 fusion.89
  134.4 9.6 %collective-permute-done.6 = bf16[512,1280]{1,0:T(8,128)(2,1)S(1)} collective-permute-done((bf16[512,1280]{1,0:T(8,128)(2,1)S(1)}, bf16[512,1280]{1,0:T(8,128)(2,1)S(1)}, u32[]{:S(2)}, u32[]{:S(2)}) %collective-permute-start.6) | collective-permute-done | bytes 1310752 | tf_op jit(solution)/shard_map/ppermute | solution.py:258
  166.0 7.2 %collective-permute-done.9 = bf16[512,1280]{1,0:T(8,128)(2,1)S(1)} collective-permute-done((bf16[512,1280]{1,0:T(8,128)(2,1)S(1)}, bf16[512,1280]{1,0:T(8,128)(2,1)S(1)}, u32[]{:S(2)}, u32[]{:S(2)}) %collective-permute-start.9) | collective-permute-done | bytes 1310752 | tf_op jit(solution)/shard_map/ppermute | solution.py:258
  173.2 3.6 collective-permute-done.11
  187.8 5.1 %fusion.56 = f32[512,1024]{1,0:T(8,128)} fusion(f32[512,1024]{1,0:T(8,128)} %add_add_fusion, bf16[512,1024]{1,0:T(8,128)(2,1)} %slice.105, bf16[8192,1024]{1,0:T(8,128)(2,1)} %param.22, s32[]{:T(128)S(6)} %select_n.338), kind=kOutput, calls=%fused_computation.84 | convolution fusion | flops 1074266112 | bytes 7340036 | tf_op jit(solution)/shard_map/dot_general | solution.py:208
  210.7 10.4 %fusion.11 = (bf16[4,1024,64]{2,1,0:T(8,128)(2,1)}, bf16[4,1024,64]{2,1,0:T(8,128)(2,1)}) fusion(f32[4,1024,128]{2,1,0:T(8,128)S(1)} %get-tuple-element.229, f32[64]{0:T(128)S(1)} %copy-done.25, f32[4,1024]{1,0:T(4,128)S(1)} %copy-done.21), kind=kLoop, calls=%fused_computation.22 | loop fusion | flops 2359296 | bytes 3162368 | tf_op jit(solution)/shard_map/convert.4
  221.1 14.3 %fusion.163 = (f32[4,1024]{1,0:T(4,128)}, bf16[4,1024,1152]{2,1,0:T(8,128)(2,1)}) fusion(pred[1024,1152]{1,0:T(8,128)(4,1)S(1)} %copy-done.13, bf16[4,128,64]{2,1,0:T(8,128)(2,1)} %get-tuple-element.270, bf16[4,128,64]{2,1,0:T(8,128)(2,1)S(1)} %get-tuple-element.269, bf16[4,1024,64]{2,1,0:T(8,128)(2,1)} %get-tuple-element.227, ...), kind=kOutput, calls=%fused_computation.220 | convolution fusion | flops 1237845120 | bytes 13910016 | tf_op jit(solution)/shard_map/vmap()/sub | solution.py:47
  235.4 6.6 %divide_convert_fusion = bf16[4,1024,128]{2,1,0:T(8,128)(2,1)S(1)} fusion(f32[4,1024]{1,0:T(4,128)} %get-tuple-element.279, bf16[4,128,128]{2,1,0:T(8,128)(2,1)S(1)} %get-tuple-element.271, bf16[4,1024,128]{2,1,0:T(8,128)(2,1)} %get-tuple-element.228, bf16[4,1024,1152]{2,1,0:T(8,128)(2,1)} %get-tuple-element.280), kind=kOutput, calls=%fused_computation.53 | convolution fusion | flops 1211367424 | bytes 11681792 | tf_op jit(solution)/shard_map/vmap()/dot_general | solution.py:49
  250.7 3.8 %fusion.62 = bf16[512,1024]{1,0:T(8,128)(2,1)} fusion(bf16[512,1024]{1,0:T(8,128)(2,1)S(1)} %bitcast.73, bf16[1024,8192]{1,0:T(8,128)(2,1)} %param.24, s32[]{:T(128)S(6)} %select_n.346), kind=kOutput, calls=%fused_computation.86 | convolution fusion | flops 1074266112 | bytes 4194308 | tf_op jit(solution)/shard_map/dot_general | solution.py:395
  254.5 16.9 %collective-permute-done.15 = bf16[512,1024]{1,0:T(8,128)(2,1)S(1)} collective-permute-done((bf16[512,1024]{1,0:T(8,128)(2,1)S(1)}, bf16[512,1024]{1,0:T(8,128)(2,1)S(1)}, u32[]{:S(2)}, u32[]{:S(2)}) %collective-permute-start.15) | collective-permute-done | bytes 1048608 | tf_op jit(solution)/shard_map/ppermute | solution.py:319
  274.9 4.4 %collective-permute-start.17 = (bf16[512,1024]{1,0:T(8,128)(2,1)S(1)}, bf16[512,1024]{1,0:T(8,128)(2,1)}, u32[]{:S(2)}, u32[]{:S(2)}) collective-permute-start(bf16[512,1024]{1,0:T(8,128)(2,1)S(1)} %get-tuple-element.186), channel_id=1, source_target_pairs={{0,4},{2,6},{1,5},{3,7},{16,20},{18,22},{17,21},{19,23}} | collective-permute-start | bytes 3145736 | tf_op jit(solution)/shard_map/ppermute | solution.py:96
  284.0 4.0 %fusion.65 = bf16[512,1024]{1,0:T(8,128)(2,1)} fusion(bf16[512,1024]{1,0:T(8,128)(2,1)S(1)} %bitcast.75, bf16[1024,8192]{1,0:T(8,128)(2,1)} %param.24, s32[]{:T(128)S(6)} %select_n.348), kind=kOutput, calls=%fused_computation.87 | convolution fusion | flops 1074266112 | bytes 4194308 | tf_op jit(solution)/shard_map/dot_general | solution.py:395
  288.0 9.9 %collective-permute-done.16 = bf16[512,1024]{1,0:T(8,128)(2,1)S(1)} collective-permute-done((bf16[512,1024]{1,0:T(8,128)(2,1)}, bf16[512,1024]{1,0:T(8,128)(2,1)S(1)}, u32[]{:S(2)}, u32[]{:S(2)}) %collective-permute-start.16) | collective-permute-done | bytes 1048608 | tf_op jit(solution)/shard_map/ppermute | solution.py:319
  303.5 5.5 %collective-permute-start.20 = (bf16[512,1024]{1,0:T(8,128)(2,1)}, bf16[512,1024]{1,0:T(8,128)(2,1)}, u32[]{:S(2)}, u32[]{:S(2)}) collective-permute-start(bf16[512,1024]{1,0:T(8,128)(2,1)} %get-tuple-element.196), channel_id=1, source_target_pairs={{0,4},{2,6},{4,8},{6,10},{1,5},{3,7},{5,9},{7,11},{16,20},{18,22},... | collective-permute-start | bytes 3145736 | tf_op jit(solution)/shard_map/ppermute | solution.py:96
  313.9 3.8 %fusion.68 = bf16[512,1024]{1,0:T(8,128)(2,1)} fusion(bf16[512,1024]{1,0:T(8,128)(2,1)S(1)} %bitcast.78, bf16[1024,8192]{1,0:T(8,128)(2,1)} %param.24, s32[]{:T(128)S(6)} %select_n.352), kind=kOutput, calls=%fused_computation.88 | convolution fusion | flops 1074266112 | bytes 4194308 | tf_op jit(solution)/shard_map/dot_general | solution.py:395
  317.7 9.1 %collective-permute-done.19 = bf16[512,1024]{1,0:T(8,128)(2,1)S(1)} collective-permute-done((bf16[512,1024]{1,0:T(8,128)(2,1)}, bf16[512,1024]{1,0:T(8,128)(2,1)S(1)}, u32[]{:S(2)}, u32[]{:S(2)}) %collective-permute-start.19) | collective-permute-done | bytes 1048608 | tf_op jit(solution)/shard_map/ppermute | solution.py:319
  336.2 9.2 %collective-permute-start.23 = (bf16[512,1024]{1,0:T(8,128)(2,1)}, bf16[512,1024]{1,0:T(8,128)(2,1)S(1)}, u32[]{:S(2)}, u32[]{:S(2)}) collective-permute-start(bf16[512,1024]{1,0:T(8,128)(2,1)} %add_convert_fusion.1), channel_id=1, source_target_pairs={{0,4},{2,6},{4,8},{6,10},{8,12},{10,14},{1,5},{3,7},{5,9},{7,11},{... | collective-permute-start | bytes 3145736 | tf_op jit(solution)/shard_map/ppermute | solution.py:96
  350.0 6.9 %collective-permute-done.22 = bf16[512,1024]{1,0:T(8,128)(2,1)S(1)} collective-permute-done((bf16[512,1024]{1,0:T(8,128)(2,1)}, bf16[512,1024]{1,0:T(8,128)(2,1)S(1)}, u32[]{:S(2)}, u32[]{:S(2)}) %collective-permute-start.22) | collective-permute-done | bytes 1048608 | tf_op jit(solution)/shard_map/ppermute | solution.py:319
  356.9 7.9 %collective-permute-done.23 = bf16[512,1024]{1,0:T(8,128)(2,1)S(1)} collective-permute-done((bf16[512,1024]{1,0:T(8,128)(2,1)}, bf16[512,1024]{1,0:T(8,128)(2,1)S(1)}, u32[]{:S(2)}, u32[]{:S(2)}) %collective-permute-start.23) | collective-permute-done | bytes 1048608 | tf_op jit(solution)/shard_map/ppermute | solution.py:96
  364.8 4.1 %collective-permute-done.24 = bf16[512,1024]{1,0:T(8,128)(2,1)S(1)} collective-permute-done((bf16[512,1024]{1,0:T(8,128)(2,1)}, bf16[512,1024]{1,0:T(8,128)(2,1)S(1)}, u32[]{:S(2)}, u32[]{:S(2)}) %collective-permute-start.24) | collective-permute-done | bytes 1048608 | tf_op jit(solution)/shard_map/ppermute | solution.py:96
  (208 shorter events, 148.1 us)
Async XLA Ops:
  7.2 200.3 %all-gather.4.cloned.1.call-start = ((), (), s32[]{:S(2)}) async-start(), calls=%async_computation | async-start | bytes 1572864 | tf_op jit(solution)/shard_map/all_gather | solution.py:381
  11.0 80.1 %collective-permute-start = (bf16[512,1024]{1,0:T(8,128)(2,1)S(1)}, bf16[512,1024]{1,0:T(8,128)(2,1)}, u32[]{:S(2)}, u32[]{:S(2)}) collective-permute-start(bf16[512,1024]{1,0:T(8,128)(2,1)S(1)} %get-tuple-element.173), channel_id=1, source_target_pairs={{0,2},{2,0},{4,6},{6,4},{8,10},{10,8},{12,14},{14,12},{1,3},{3,1},... | collective-permute-start | bytes 3145736 | tf_op jit(solution)/shard_map/ppermute | solution.py:258
  14.0 77.1 %collective-permute-start.1 = (bf16[512,1024]{1,0:T(8,128)(2,1)S(1)}, bf16[512,1024]{1,0:T(8,128)(2,1)S(1)}, u32[]{:S(2)}, u32[]{:S(2)}) collective-permute-start(bf16[512,1024]{1,0:T(8,128)(2,1)S(1)} %get-tuple-element.173), channel_id=1, source_target_pairs={{0,4},{2,6},{4,8},{6,10},{8,12},{10,14},{1,5},{3,7},{5,9},{7,11},{... | collective-permute-start | bytes 3145736 | tf_op jit(solution)/shard_map/ppermute | solution.py:96
  17.5 73.6 %collective-permute-start.2 = (bf16[512,1024]{1,0:T(8,128)(2,1)S(1)}, bf16[512,1024]{1,0:T(8,128)(2,1)S(1)}, u32[]{:S(2)}, u32[]{:S(2)}) collective-permute-start(bf16[512,1024]{1,0:T(8,128)(2,1)S(1)} %get-tuple-element.173), channel_id=1, source_target_pairs={{4,0},{6,2},{8,4},{10,6},{12,8},{14,10},{5,1},{7,3},{9,5},{11,7},{... | collective-permute-start | bytes 3145736 | tf_op jit(solution)/shard_map/ppermute | solution.py:96
  92.3 25.0 %collective-permute-start.3 = (bf16[512,1280]{1,0:T(8,128)(2,1)S(1)}, bf16[512,1280]{1,0:T(8,128)(2,1)S(1)}, u32[]{:S(2)}, u32[]{:S(2)}) collective-permute-start(bf16[512,1280]{1,0:T(8,128)(2,1)S(1)} %pad_maximum_fusion.4), channel_id=1, source_target_pairs={{0,2},{2,0},{4,6},{6,4},{8,10},{10,8},{12,14},{14,12},{1,3},{3,1},... | collective-permute-start | bytes 3932168 | tf_op jit(solution)/shard_map/ppermute | solution.py:258
  92.4 17.2 %collective-permute-start.4 = (bf16[512,1024]{1,0:T(8,128)(2,1)S(1)}, bf16[512,1024]{1,0:T(8,128)(2,1)S(1)}, u32[]{:S(2)}, u32[]{:S(2)}) collective-permute-start(bf16[512,1024]{1,0:T(8,128)(2,1)S(1)} %get-tuple-element.120), channel_id=1, source_target_pairs={{0,4},{2,6},{4,8},{6,10},{8,12},{10,14},{1,5},{3,7},{5,9},{7,11},{... | collective-permute-start | bytes 3145736 | tf_op jit(solution)/shard_map/ppermute | solution.py:96
  94.0 20.0 %collective-permute-start.5 = (bf16[512,1024]{1,0:T(8,128)(2,1)S(1)}, bf16[512,1024]{1,0:T(8,128)(2,1)S(1)}, u32[]{:S(2)}, u32[]{:S(2)}) collective-permute-start(bf16[512,1024]{1,0:T(8,128)(2,1)S(1)} %get-tuple-element.121), channel_id=1, source_target_pairs={{4,0},{6,2},{8,4},{10,6},{12,8},{14,10},{5,1},{7,3},{9,5},{11,7},{... | collective-permute-start | bytes 3145736 | tf_op jit(solution)/shard_map/ppermute | solution.py:96
  121.3 22.6 %collective-permute-start.6 = (bf16[512,1280]{1,0:T(8,128)(2,1)S(1)}, bf16[512,1280]{1,0:T(8,128)(2,1)S(1)}, u32[]{:S(2)}, u32[]{:S(2)}) collective-permute-start(bf16[512,1280]{1,0:T(8,128)(2,1)S(1)} %pad_maximum_fusion.5), channel_id=1, source_target_pairs={{0,2},{2,0},{4,6},{6,4},{8,10},{10,8},{12,14},{14,12},{1,3},{3,1},... | collective-permute-start | bytes 3932168 | tf_op jit(solution)/shard_map/ppermute | solution.py:258
  121.3 22.6 %collective-permute-start.7 = (bf16[512,1280]{1,0:T(8,128)(2,1)}, bf16[512,1280]{1,0:T(8,128)(2,1)S(1)}, u32[]{:S(2)}, u32[]{:S(2)}) collective-permute-start(bf16[512,1280]{1,0:T(8,128)(2,1)} %get-tuple-element.136), channel_id=1, source_target_pairs={{0,4},{2,6},{4,8},{6,10},{8,12},{10,14},{1,5},{3,7},{5,9},{7,11},{... | collective-permute-start | bytes 3932168 | tf_op jit(solution)/shard_map/ppermute | solution.py:96
  122.8 23.5 %collective-permute-start.8 = (bf16[512,1280]{1,0:T(8,128)(2,1)}, bf16[512,1280]{1,0:T(8,128)(2,1)S(1)}, u32[]{:S(2)}, u32[]{:S(2)}) collective-permute-start(bf16[512,1280]{1,0:T(8,128)(2,1)} %get-tuple-element.137), channel_id=1, source_target_pairs={{4,0},{6,2},{8,4},{10,6},{12,8},{14,10},{5,1},{7,3},{9,5},{11,7},{... | collective-permute-start | bytes 3932168 | tf_op jit(solution)/shard_map/ppermute | solution.py:96
  151.8 21.4 %collective-permute-start.9 = (bf16[512,1280]{1,0:T(8,128)(2,1)S(1)}, bf16[512,1280]{1,0:T(8,128)(2,1)S(1)}, u32[]{:S(2)}, u32[]{:S(2)}) collective-permute-start(bf16[512,1280]{1,0:T(8,128)(2,1)S(1)} %pad_maximum_fusion.6), channel_id=1, source_target_pairs={{0,2},{2,0},{4,6},{6,4},{8,10},{10,8},{12,14},{14,12},{1,3},{3,1},... | collective-permute-start | bytes 3932168 | tf_op jit(solution)/shard_map/ppermute | solution.py:258
  153.2 20.0 %collective-permute-start.10 = (bf16[512,1280]{1,0:T(8,128)(2,1)S(1)}, bf16[512,1280]{1,0:T(8,128)(2,1)S(1)}, u32[]{:S(2)}, u32[]{:S(2)}) collective-permute-start(bf16[512,1280]{1,0:T(8,128)(2,1)S(1)} %get-tuple-element.153), channel_id=1, source_target_pairs={{0,4},{2,6},{4,8},{6,10},{8,12},{10,14},{1,5},{3,7},{5,9},{7,11},{... | collective-permute-start | bytes 3932168 | tf_op jit(solution)/shard_map/ppermute | solution.py:96
  155.4 21.4 %collective-permute-start.11 = (bf16[512,1280]{1,0:T(8,128)(2,1)S(1)}, bf16[512,1280]{1,0:T(8,128)(2,1)S(1)}, u32[]{:S(2)}, u32[]{:S(2)}) collective-permute-start(bf16[512,1280]{1,0:T(8,128)(2,1)S(1)} %get-tuple-element.154), channel_id=1, source_target_pairs={{4,0},{6,2},{8,4},{10,6},{12,8},{14,10},{5,1},{7,3},{9,5},{11,7},{... | collective-permute-start | bytes 3932168 | tf_op jit(solution)/shard_map/ppermute | solution.py:96
  180.5 15.4 %collective-permute-start.12 = (bf16[512,768]{1,0:T(8,128)(2,1)}, bf16[512,768]{1,0:T(8,128)(2,1)}, u32[]{:S(2)}, u32[]{:S(2)}) collective-permute-start(bf16[512,768]{1,0:T(8,128)(2,1)} %pad_maximum_fusion.10), channel_id=1, source_target_pairs={{0,2},{2,0},{4,6},{6,4},{8,10},{10,8},{12,14},{14,12},{1,3},{3,1},... | collective-permute-start | bytes 2359304 | tf_op jit(solution)/shard_map/ppermute | solution.py:258
  246.2 25.2 %collective-permute-start.15 = (bf16[512,1024]{1,0:T(8,128)(2,1)S(1)}, bf16[512,1024]{1,0:T(8,128)(2,1)S(1)}, u32[]{:S(2)}, u32[]{:S(2)}) collective-permute-start(bf16[512,1024]{1,0:T(8,128)(2,1)S(1)} %fusion.59), channel_id=1, source_target_pairs={{0,2},{2,0},{4,6},{6,4},{8,10},{10,8},{12,14},{14,12},{1,3},{3,1},... | collective-permute-start | bytes 3145736 | tf_op jit(solution)/shard_map/ppermute | solution.py:319
  273.2 24.8 %collective-permute-start.16 = (bf16[512,1024]{1,0:T(8,128)(2,1)}, bf16[512,1024]{1,0:T(8,128)(2,1)S(1)}, u32[]{:S(2)}, u32[]{:S(2)}) collective-permute-start(bf16[512,1024]{1,0:T(8,128)(2,1)} %fusion.62), channel_id=1, source_target_pairs={{0,2},{2,0},{4,6},{6,4},{8,10},{10,8},{12,14},{14,12},{1,3},{3,1},... | collective-permute-start | bytes 3145736 | tf_op jit(solution)/shard_map/ppermute | solution.py:319
  274.9 25.2 %collective-permute-start.17 = (bf16[512,1024]{1,0:T(8,128)(2,1)S(1)}, bf16[512,1024]{1,0:T(8,128)(2,1)}, u32[]{:S(2)}, u32[]{:S(2)}) collective-permute-start(bf16[512,1024]{1,0:T(8,128)(2,1)S(1)} %get-tuple-element.186), channel_id=1, source_target_pairs={{0,4},{2,6},{1,5},{3,7},{16,20},{18,22},{17,21},{19,23}} | collective-permute-start | bytes 3145736 | tf_op jit(solution)/shard_map/ppermute | solution.py:96
  279.3 20.8 %collective-permute-start.18 = (bf16[512,1024]{1,0:T(8,128)(2,1)S(1)}, bf16[512,1024]{1,0:T(8,128)(2,1)}, u32[]{:S(2)}, u32[]{:S(2)}) collective-permute-start(bf16[512,1024]{1,0:T(8,128)(2,1)S(1)} %get-tuple-element.186), channel_id=1, source_target_pairs={{12,8},{14,10},{13,9},{15,11},{28,24},{30,26},{29,25},{31,27}} | collective-permute-start | bytes 3145736 | tf_op jit(solution)/shard_map/ppermute | solution.py:96
  303.2 23.6 %collective-permute-start.19 = (bf16[512,1024]{1,0:T(8,128)(2,1)}, bf16[512,1024]{1,0:T(8,128)(2,1)S(1)}, u32[]{:S(2)}, u32[]{:S(2)}) collective-permute-start(bf16[512,1024]{1,0:T(8,128)(2,1)} %fusion.65), channel_id=1, source_target_pairs={{0,2},{2,0},{4,6},{6,4},{8,10},{10,8},{12,14},{14,12},{1,3},{3,1},... | collective-permute-start | bytes 3145736 | tf_op jit(solution)/shard_map/ppermute | solution.py:319
  303.5 25.4 %collective-permute-start.20 = (bf16[512,1024]{1,0:T(8,128)(2,1)}, bf16[512,1024]{1,0:T(8,128)(2,1)}, u32[]{:S(2)}, u32[]{:S(2)}) collective-permute-start(bf16[512,1024]{1,0:T(8,128)(2,1)} %get-tuple-element.196), channel_id=1, source_target_pairs={{0,4},{2,6},{4,8},{6,10},{1,5},{3,7},{5,9},{7,11},{16,20},{18,22},... | collective-permute-start | bytes 3145736 | tf_op jit(solution)/shard_map/ppermute | solution.py:96
  309.0 19.9 %collective-permute-start.21 = (bf16[512,1024]{1,0:T(8,128)(2,1)}, bf16[512,1024]{1,0:T(8,128)(2,1)}, u32[]{:S(2)}, u32[]{:S(2)}) collective-permute-start(bf16[512,1024]{1,0:T(8,128)(2,1)} %get-tuple-element.196), channel_id=1, source_target_pairs={{8,4},{10,6},{12,8},{14,10},{9,5},{11,7},{13,9},{15,11},{24,20},{2... | collective-permute-start | bytes 3145736 | tf_op jit(solution)/shard_map/ppermute | solution.py:96
  334.5 22.4 %collective-permute-start.22 = (bf16[512,1024]{1,0:T(8,128)(2,1)}, bf16[512,1024]{1,0:T(8,128)(2,1)S(1)}, u32[]{:S(2)}, u32[]{:S(2)}) collective-permute-start(bf16[512,1024]{1,0:T(8,128)(2,1)} %fusion.68), channel_id=1, source_target_pairs={{0,2},{2,0},{4,6},{6,4},{8,10},{10,8},{12,14},{14,12},{1,3},{3,1},... | collective-permute-start | bytes 3145736 | tf_op jit(solution)/shard_map/ppermute | solution.py:319
  336.2 28.5 %collective-permute-start.23 = (bf16[512,1024]{1,0:T(8,128)(2,1)}, bf16[512,1024]{1,0:T(8,128)(2,1)S(1)}, u32[]{:S(2)}, u32[]{:S(2)}) collective-permute-start(bf16[512,1024]{1,0:T(8,128)(2,1)} %add_convert_fusion.1), channel_id=1, source_target_pairs={{0,4},{2,6},{4,8},{6,10},{8,12},{10,14},{1,5},{3,7},{5,9},{7,11},{... | collective-permute-start | bytes 3145736 | tf_op jit(solution)/shard_map/ppermute | solution.py:96
  345.4 23.4 %collective-permute-start.24 = (bf16[512,1024]{1,0:T(8,128)(2,1)}, bf16[512,1024]{1,0:T(8,128)(2,1)S(1)}, u32[]{:S(2)}, u32[]{:S(2)}) collective-permute-start(bf16[512,1024]{1,0:T(8,128)(2,1)} %get-tuple-element.206), channel_id=1, source_target_pairs={{4,0},{6,2},{8,4},{10,6},{12,8},{14,10},{5,1},{7,3},{9,5},{11,7},{... | collective-permute-start | bytes 3145736 | tf_op jit(solution)/shard_map/ppermute | solution.py:96
  (37 other events, 471.5 us)
Sparse Core Ops, SparseCore 0:
  198.9 8.3 all-gather.3
